TPU v7x, 32 devices: a whole 2x2x4 slice. The times are simulated.
32 devices in a mesh: dp: 4 (over y, x), tensor: 8 (over z, core).
Axes of the slice: x: 2, y: 2, z: 4, core: 2. Of those that a mesh axis runs over, the one named last changes fastest.
Arguments:
- tokens: bfloat16 [1024, 8192], P('dp'), may hold values from -6 to 6
- out_grad: bfloat16 [1024, 8192], P('dp'), may hold values from -6 to 6
- weight_tiles: bfloat16 [256, 2, 3, 128, 128], P(('dp', 'tensor')), may hold values from -0.125 to 0.125
- tile_places: int32 [256, 2], P(('dp', 'tensor')), may hold values from 0 to 1663, as said below
- live_counts: int32 [256], P(('dp', 'tensor')), may hold values from 0 to 2, as said below
Outputs:
- layer_out: bfloat16 [1024, 8192], P('dp', 'tensor')
- input_grad: bfloat16 [1024, 8192], P('dp', 'tensor')
Inputs may be any that keep to these rules, and one draw needn't show every extreme that they name: `tile_places`: among the slots addressed to one owner, live or not, no two have the same place; the place 64 * 26 - 1 occurs in a live slot of every owner. `live_counts`: every owner receives 2 live slots from some source, and some owner receives 2 live slots from every source; slots past the count hold padding.
All inputs are finite; a program needn't handle non-finite values.
Results may differ from a plain program's by a relative error of at most 0.012.
Values may be sent and summed in bfloat16 or wider, within the bound.
A program may use at most 192 MiB of HBM per device.

v0:
```python
import jax
import jax.numpy as jnp
from jax import lax
from jax.sharding import PartitionSpec as P

FF = 26624


def block_length(extent):
    length = min(extent, 32)
    while extent % length:
        length -= 1
    return length


def over_blocks(step, running, arrays):
    extent = arrays[0].shape[0]
    length = block_length(extent)
    shaped = tuple((item.reshape((extent // length, length) + item.shape[1:]) for item in arrays))

    def advance(acc_value, slot_block):
        return (step(acc_value, slot_block), None)

    running, _ = lax.scan(advance, running, shaped)
    return running


def body(tokens, out_grad, weight_tiles, tile_places, live_counts):
    tok_rows = tokens.shape[0]
    feat_width = tokens.shape[1]
    tile_side = weight_tiles.shape[-1]
    peer_slots = weight_tiles.shape[1]
    row_count = feat_width // tile_side
    owners = lax.axis_size("tensor")
    col_count = FF // (tile_side * owners)
    arrived_tiles, arrived_places, arrived_counts = (
        lax.all_to_all(weight_tiles, "tensor", split_axis=0, concat_axis=0, tiled=True),
        lax.all_to_all(tile_places, "tensor", split_axis=0, concat_axis=0, tiled=True),
        lax.all_to_all(live_counts, "tensor", split_axis=0, concat_axis=0, tiled=True),
    )
    slot_tiles, slot_places, slot_counts = (
        lax.all_gather(arrived_tiles, "dp", axis=0, tiled=True),
        lax.all_gather(arrived_places, "dp", axis=0, tiled=True),
        lax.all_gather(arrived_counts, "dp", axis=0, tiled=True),
    )
    slot_total = slot_places.shape[0] * peer_slots
    row_ids = (slot_places // col_count).reshape(-1).astype(jnp.int32)
    col_ids = (slot_places % col_count).reshape(-1).astype(jnp.int32)
    live_mask = (jnp.arange(peer_slots)[None, :] < slot_counts[:, None]).reshape(-1)
    flat_tiles = slot_tiles.reshape((slot_total,) + slot_tiles.shape[2:])
    flat_tiles = jnp.where(
        live_mask[:, None, None, None], flat_tiles, jnp.zeros((), flat_tiles.dtype)
    )
    slot_data = (flat_tiles, row_ids, col_ids)
    token_blocks = tokens.reshape(tok_rows, row_count, tile_side)

    def gate_up_step(acc_value, slot_block):
        weights, row_block, col_block = slot_block
        gathered = jnp.take(token_blocks, row_block, axis=1)
        products = jnp.einsum(
            "tsa,sgab->gtsb", gathered, weights[:, 0:2], preferred_element_type=jnp.float32
        )
        return acc_value.at[:, :, col_block, :].add(products)

    preact = over_blocks(
        gate_up_step, jnp.zeros((2, tok_rows, col_count, tile_side), jnp.float32), slot_data
    )
    gate_pre = preact[0]
    up_pre = preact[1]
    sigmoid_gate = jax.nn.sigmoid(gate_pre)
    gate_act = gate_pre * sigmoid_gate
    hidden = (gate_act * up_pre).astype(jnp.bfloat16)

    def down_step(acc_value, slot_block):
        weights, row_block, col_block = slot_block
        gathered = jnp.take(hidden, col_block, axis=1)
        products = jnp.einsum(
            "tsa,sab->tsb", gathered, weights[:, 2], preferred_element_type=jnp.float32
        )
        return acc_value.at[:, row_block, :].add(products)

    out_part = over_blocks(
        down_step, jnp.zeros((tok_rows, row_count, tile_side), jnp.float32), slot_data
    ).reshape(tok_rows, feat_width)
    layer_out = lax.psum_scatter(
        out_part.astype(jnp.bfloat16), "tensor", scatter_dimension=1, tiled=True
    )
    grad_blocks = out_grad.reshape(tok_rows, row_count, tile_side)

    def back_step(acc_value, slot_block):
        weights, row_block, col_block = slot_block
        gathered = jnp.take(grad_blocks, row_block, axis=1)
        products = jnp.einsum(
            "tsb,sab->tsa", gathered, weights[:, 2], preferred_element_type=jnp.float32
        )
        return acc_value.at[:, col_block, :].add(products)

    grad_hidden = over_blocks(
        back_step, jnp.zeros((tok_rows, col_count, tile_side), jnp.float32), slot_data
    )
    grad_gate = (
        grad_hidden * up_pre * (sigmoid_gate * (1.0 + gate_pre * (1.0 - sigmoid_gate)))
    ).astype(jnp.bfloat16)
    grad_up = (grad_hidden * gate_act).astype(jnp.bfloat16)
    grad_pair = jnp.stack([grad_gate, grad_up])

    def input_step(acc_value, slot_block):
        weights, row_block, col_block = slot_block
        gathered = jnp.take(grad_pair, col_block, axis=2)
        products = jnp.einsum(
            "gtsb,sgab->tsa", gathered, weights[:, 0:2], preferred_element_type=jnp.float32
        )
        return acc_value.at[:, row_block, :].add(products)

    in_part = over_blocks(
        input_step, jnp.zeros((tok_rows, row_count, tile_side), jnp.float32), slot_data
    ).reshape(tok_rows, feat_width)
    input_grad = lax.psum_scatter(
        in_part.astype(jnp.bfloat16), "tensor", scatter_dimension=1, tiled=True
    )
    return (layer_out, input_grad)


def solution(mesh):
    in_specs = (
        P("dp", None),
        P("dp", None),
        P(("dp", "tensor"), None, None, None, None),
        P(("dp", "tensor"), None),
        P(("dp", "tensor")),
    )
    out_specs = (P("dp", "tensor"), P("dp", "tensor"))
    return jax.shard_map(body, mesh=mesh, in_specs=in_specs, out_specs=out_specs, check_vma=False)
```

profile of v0, /device:TPU:0, one launch (start us, length us, event | category | flops | bytes accessed | tf_op | source)
XLA Modules:
  0.0 404.7 jit_solution(2578205139297796959)
XLA Ops:
  7.2 44.3 %all_to_all.29 = bf16[8,2,3,128,128]{4,3,2,1,0:T(8,128)(2,1)} all-to-all(bf16[8,2,3,128,128]{4,3,2,1,0:T(8,128)(2,1)} %param.17), channel_id=1, replica_groups=mesh['dp'=4,'tensor'=8] {'tensor'}, dimensions={0} | all-to-all | bytes 3145728 | tf_op jit(solution)/shard_map/all_to_all | solution.py:37
  56.3 6.7 %copy.90 = bf16[256,8192]{0,1:T(8,128)(2,1)} copy(bf16[256,8192]{1,0:T(8,128)(2,1)} %param.16) | data formatting | bytes 8388608 | tf_op args[1]
  63.0 6.4 %copy.92 = bf16[256,64,128]{2,0,1:T(8,128)(2,1)} copy(bf16[256,64,128]{0,2,1:T(8,128)(2,1)} %bitcast.209) | data formatting | bytes 8388608 | tf_op jit(solution)/shard_map/while | solution.py:24
  75.8 6.4 %copy.87 = bf16[256,64,128]{2,0,1:T(8,128)(2,1)} copy(bf16[256,64,128]{0,2,1:T(8,128)(2,1)} %bitcast.210) | data formatting | bytes 8388608 | tf_op jit(solution)/shard_map/while | solution.py:24
  88.9 7.5 %all-reduce = s32[32]{0:T(128)S(1)} all-reduce(s32[32]{0:T(128)S(1)} %dynamic-update-slice), channel_id=3, replica_groups=mesh['dp'=4,'tensor'=8] {'dp'}, use_global_device_ids=true, to_apply=%add | all-reduce | flops 32 | bytes 256
  96.7 8.3 %all-gather = s32[32,1,2]{2,1,0:T(1,128)S(1)} all-gather(s32[8,1,2]{2,1,0:T(1,128)S(1)} %all-to-all-done), channel_id=2, replica_groups=mesh['dp'=4,'tensor'=8] {'dp'}, dimensions={0}, use_global_device_ids=true | all-gather | bytes 320 | tf_op jit(solution)/shard_map/all_gather | solution.py:43
  105.5 15.5 %all-gather.4.cloned.1.call-done = bf16[32,2,3,128,128]{4,3,2,1,0:T(8,128)(2,1)} async-done(((bf16[8,2,3,128,128]{4,3,2,1,0:T(8,128)(2,1)}), bf16[32,2,3,128,128]{4,3,2,1,0:T(8,128)(2,1)}) %all-gather.4.cloned.1.call-update) | async-done | bytes 6291472 | tf_op jit(solution)/shard_map/all_gather | solution.py:42
  129.2 32.5 %while.42 = (s32[]{:T(128)}, f32[256,26,128]{2,0,1:T(8,128)S(1)}, s32[2,32]{1,0:T(2,128)S(1)}, bf16[2,32,3,128,128]{4,3,1,2,0:T(8,128)(2,1)}, s32[2,32]{1,0:T(2,...) while((s32[]{:T(128)}, f32[256,26,128]{2,0,1:T(8,128)S(1)}, s32[2,32]{1,0:T(2,128)S(1)}, ...), condition=%wide.region_9.11_spmd, body=%wide.region_7.10_spmd.sunk | while | flops 270533920 | bytes 38802964 | solution.py:24
  139.0 6.5 %scatter_fusion.2 = f32[256,26,128]{2,0,1:T(8,128)S(1)} fusion(f32[256,26,128]{2,0,1:T(8,128)S(1)} %get-tuple-element.497, s32[32]{0:T(128)S(1)} %fusion.73, f32[32,256,128]{2,1,0:T(8,128)} %fusion.74), kind=kCustom, calls=%fused_computation.7.clone.1 | custom fusion | flops 1048576 | bytes 12583040 | tf_op jit(solution)/shard_map/while/body/eval_jaxpr/scatter-add | solution.py:96
  155.1 6.5 %scatter_fusion.2 = f32[256,26,128]{2,0,1:T(8,128)S(1)} fusion(f32[256,26,128]{2,0,1:T(8,128)S(1)} %get-tuple-element.497, s32[32]{0:T(128)S(1)} %fusion.73, f32[32,256,128]{2,1,0:T(8,128)} %fusion.74), kind=kCustom, calls=%fused_computation.7.clone.1 | custom fusion | flops 1048576 | bytes 12583040 | tf_op jit(solution)/shard_map/while/body/eval_jaxpr/scatter-add | solution.py:96
  165.2 77.5 %while.40 = (s32[]{:T(128)}, f32[2,256,26,128]{3,1,2,0:T(8,128)}, s32[2,32]{1,0:T(2,128)S(1)}, bf16[2,32,3,128,128]{4,3,2,1,0:T(8,128)(2,1)}, s32[2,32]{1,0:T(2,...) while((s32[]{:T(128)}, f32[2,256,26,128]{3,1,2,0:T(8,128)}, s32[2,32]{1,0:T(2,128)S(1)}, ...), condition=%wide.region_2.4_spmd, body=%wide.region_0.3_spmd.sunk | while | flops 540017984 | bytes 59774484 | solution.py:24
  169.6 6.8 %convolution_bitcast_fusion.2 = f32[32,2,256,128]{2,3,1,0:T(8,128)} fusion(bf16[2,32,3,128,128]{4,3,2,1,0:T(8,128)(2,1)} %get-tuple-element.485, s32[]{:T(128)} %get-tuple-element.475, bf16[32,256,128]{2,1,0:T(8,128)(2,1)} %gather_fusion, pred[32]{0:T(512)(128)(4,1)S(1)} %get-tuple-element.443), kind=kOutput, calls=%fused_computation.45.clone.1 | convolution fusion | flops 537919488 | bytes 13632032 | tf_op jit(solution)/shard_map/while/body/eval_jaxpr/tsa,sgab->gtsb/dot_general | solution.py:60
  176.4 9.0 %copy.102 = f32[32,2,256,128]{3,2,1,0:T(8,128)} copy(f32[32,2,256,128]{2,3,1,0:T(8,128)} %convolution_bitcast_fusion.2) | data formatting | bytes 16777216 | tf_op jit(solution)/shard_map/while/body/eval_jaxpr/tsa,sgab->gtsb/transpose | solution.py:60
  185.4 18.7 %scatter_fusion = f32[2,256,26,128]{3,1,2,0:T(8,128)} fusion(f32[2,256,26,128]{3,1,2,0:T(8,128)} %get-tuple-element.476, s32[32]{0:T(128)S(1)} %fusion.68, f32[32,2,256,128]{3,2,1,0:T(8,128)} %copy.102), kind=kCustom, calls=%fused_computation.4.clone.1 | custom fusion | flops 2097152 | bytes 25165952 | tf_op jit(solution)/shard_map/while/body/eval_jaxpr/scatter-add | solution.py:63
  208.4 6.8 %convolution_bitcast_fusion.2 = f32[32,2,256,128]{2,3,1,0:T(8,128)} fusion(bf16[2,32,3,128,128]{4,3,2,1,0:T(8,128)(2,1)} %get-tuple-element.485, s32[]{:T(128)} %get-tuple-element.475, bf16[32,256,128]{2,1,0:T(8,128)(2,1)} %gather_fusion, pred[32]{0:T(512)(128)(4,1)S(1)} %get-tuple-element.443), kind=kOutput, calls=%fused_computation.45.clone.1 | convolution fusion | flops 537919488 | bytes 13632032 | tf_op jit(solution)/shard_map/while/body/eval_jaxpr/tsa,sgab->gtsb/dot_general | solution.py:60
  215.2 9.0 %copy.102 = f32[32,2,256,128]{3,2,1,0:T(8,128)} copy(f32[32,2,256,128]{2,3,1,0:T(8,128)} %convolution_bitcast_fusion.2) | data formatting | bytes 16777216 | tf_op jit(solution)/shard_map/while/body/eval_jaxpr/tsa,sgab->gtsb/transpose | solution.py:60
  224.2 18.6 %scatter_fusion = f32[2,256,26,128]{3,1,2,0:T(8,128)} fusion(f32[2,256,26,128]{3,1,2,0:T(8,128)} %get-tuple-element.476, s32[32]{0:T(128)S(1)} %fusion.68, f32[32,2,256,128]{3,2,1,0:T(8,128)} %copy.102), kind=kCustom, calls=%fused_computation.4.clone.1 | custom fusion | flops 2097152 | bytes 25165952 | tf_op jit(solution)/shard_map/while/body/eval_jaxpr/scatter-add | solution.py:63
  252.3 39.0 %while.43 = (s32[]{:T(128)}, f32[256,64,128]{2,0,1:T(8,128)}, s32[2,32]{1,0:T(2,128)S(1)}, bf16[2,32,3,128,128]{4,3,2,1,0:T(8,128)(2,1)}, s32[2,32]{1,0:T(2,128)...) while((s32[]{:T(128)}, f32[256,64,128]{2,0,1:T(8,128)}, s32[2,32]{1,0:T(2,128)S(1)}, ...), condition=%wide.region_12.14_spmd, body=%wide.region_10.13_spmd.sunk | while | flops 540018048 | bytes 54531732 | solution.py:24
  261.7 10.1 %scatter_fusion.3 = f32[256,64,128]{2,0,1:T(8,128)} fusion(f32[256,64,128]{2,0,1:T(8,128)} %get-tuple-element.539, s32[32]{0:T(128)S(1)} %get-tuple-element.466, f32[32,256,128]{2,1,0:T(8,128)} %fusion.78), kind=kCustom, calls=%fused_computation.6.clone.1 | custom fusion | flops 1048576 | bytes 12583040 | tf_op jit(solution)/shard_map/while/body/eval_jaxpr/scatter-add | solution.py:113
  281.3 10.0 %scatter_fusion.3 = f32[256,64,128]{2,0,1:T(8,128)} fusion(f32[256,64,128]{2,0,1:T(8,128)} %get-tuple-element.539, s32[32]{0:T(128)S(1)} %get-tuple-element.466, f32[32,256,128]{2,1,0:T(8,128)} %fusion.78), kind=kCustom, calls=%fused_computation.6.clone.1 | custom fusion | flops 1048576 | bytes 12583040 | tf_op jit(solution)/shard_map/while/body/eval_jaxpr/scatter-add | solution.py:113
  301.8 35.5 %while.41 = (s32[]{:T(128)}, f32[256,64,128]{2,0,1:T(8,128)}, s32[2,32]{1,0:T(2,128)S(1)}, bf16[2,32,3,128,128]{4,3,1,2,0:T(8,128)(2,1)}, s32[2,32]{1,0:T(2,128)S(1)}, /*index=5*/bf16[256,26,128]{2,0,1:T(8,128)(2,1)}, s32[]{:T(128)}) while((s32[]{:T(128)}, f32[256,64,128]{2,0,1:T(8,128)}, s32[2,32]{1,0:T(2,128)S(1)}, ...), condition=%wide.region_5.7_spmd, body=%wide.region_3.6_spmd.sunk | while | flops 270534016 | bytes 30414456 | solution.py:24
  309.4 10.2 %scatter_fusion.1 = f32[256,64,128]{2,0,1:T(8,128)} fusion(f32[256,64,128]{2,0,1:T(8,128)} %get-tuple-element.518, s32[32]{0:T(128)S(1)} %get-tuple-element.450, f32[32,256,128]{2,1,0:T(8,128)} %fusion.71), kind=kCustom, calls=%fused_computation.5.clone.1 | custom fusion | flops 1048576 | bytes 12583040 | tf_op jit(solution)/shard_map/while/body/eval_jaxpr/scatter-add | solution.py:80
  327.1 10.1 %scatter_fusion.1 = f32[256,64,128]{2,0,1:T(8,128)} fusion(f32[256,64,128]{2,0,1:T(8,128)} %get-tuple-element.518, s32[32]{0:T(128)S(1)} %get-tuple-element.450, f32[32,256,128]{2,1,0:T(8,128)} %fusion.71), kind=kCustom, calls=%fused_computation.5.clone.1 | custom fusion | flops 1048576 | bytes 12583040 | tf_op jit(solution)/shard_map/while/body/eval_jaxpr/scatter-add | solution.py:80
  347.2 51.0 %reduce-scatter.3.cloned.1.call-done = bf16[256,1024]{1,0:T(8,128)(2,1)} async-done(((bf16[256,8192]{1,0:T(8,128)(2,1)}), bf16[256,1024]{1,0:T(8,128)(2,1)}) %reduce-scatter.3.cloned.1.call-update) | async-done | bytes 524304 | tf_op jit(solution)/shard_map/reduce_scatter | solution.py:85
  (100 shorter events, 121.6 us)
Async XLA Ops:
  7.2 44.4 %copy-start.4 = (s32[8]{0:T(128)S(1)}, s32[8]{0:T(128)}, u32[]{:S(2)}) copy-start(s32[8]{0:T(128)} %param.19) | copy-start | bytes 100
  7.2 48.4 %copy-start.3 = (s32[8,2]{0,1:T(2,128)S(1)}, s32[8,2]{0,1:T(2,128)}, u32[]{:S(2)}) copy-start(s32[8,2]{0,1:T(2,128)} %param.18) | copy-start | bytes 196
  7.2 113.8 %all-gather.4.cloned.1.call-start = ((), (), s32[]{:S(2)}) async-start(), calls=%async_computation.5 | async-start | bytes 7864320 | tf_op jit(solution)/shard_map/all_gather | solution.py:42
  52.2 31.2 %all-to-all-start.1 = ((s32[8,1,1]{2,1,0:T(1,128)}), s32[8,1,1]{2,1,0:T(1,128)S(1)}, u32[]{:S(2)}, u32[]{:S(2)}) async-start(s32[8,1,1]{2,1,0:T(1,128)} %copy.83), calls=%async_computation.1 | async-start | bytes 8192 | tf_op jit(solution)/shard_map/all_to_all | solution.py:39
  75.8 6.4 %copy-start.5 = (u32[32]{0:T(128)S(1)}, u32[32]{0:T(128)}, u32[]{:S(2)}) copy-start(u32[32]{0:T(128)} %constant.120) | copy-start | bytes 388
  83.4 13.3 %all-to-all-start = ((s32[8,1,2]{2,1,0:T(1,128)}), s32[8,1,2]{2,1,0:T(1,128)S(1)}, u32[]{:S(2)}, u32[]{:S(2)}) async-start(s32[8,1,2]{2,1,0:T(1,128)} %copy.78), calls=%async_computation | async-start | bytes 8192 | tf_op jit(solution)/shard_map/all_to_all | solution.py:38
  88.4 258.8 %reduce-scatter.5.cloned.1.call-start = ((), (), s32[]{:S(2)}) async-start(), calls=%async_computation.7 | async-start | bytes 4718592 | tf_op jit(solution)/shard_map/reduce_scatter | solution.py:118
  124.3 4.5 %copy-start = (bf16[2,32,3,128,128]{4,3,2,1,0:T(8,128)(2,1)}, bf16[2,32,3,128,128]{4,3,2,1,0:T(8,128)(2,1)S(1)}, u32[]{:S(2)}) copy-start(bf16[2,32,3,128,128]{4,3,2,1,0:T(8,128)(2,1)S(1)} %bitcast_select_fusion) | copy-start | bytes 18874372
  133.7 2.5 copy-start.1
  149.9 2.5 copy-start.1
  255.3 3.1 copy-start.2
  274.9 3.1 copy-start.2
  297.2 101.0 %reduce-scatter.3.cloned.1.call-start = ((), (), s32[]{:S(2)}) async-start(), calls=%async_computation.6 | async-start | bytes 4718592 | tf_op jit(solution)/shard_map/reduce_scatter | solution.py:85
Sparse Core Ops, SparseCore 0:
  51.6 69.3 all-gather.3
  297.4 49.7 reduce-scatter.4
  350.0 48.1 reduce-scatter.2
where the time goes:
time: 407 us; the launch traced here: 405 us
  other arithmetic  112 us (28%)
  local copies, waits for them, and re-layouts  108 us (27%)
  waiting for transfers between devices  70.5 us (17%)
  blocking collectives  60.1 us (15%)
  matrix products  30.9 us (8%)
  between operations  14.5 us (4%)
  starting transfers between devices  8.66 us (2%)
    reduce_scatter x1, waiting for transfers between devices, body(): lax.psum_scatter(out_part.astype(jnp.bfloat16), 'tensor', scatter_dimensi...  51 us
    all_to_all x1, blocking collectives, body(): lax.all_to_all(weight_tiles, 'tensor', split_axis=0, concat_axis=0, tiled...  44.3 us
    scatter-add x2, other arithmetic, gate_up_step(): return acc_value.at[:, :, col_block, :].add(products)  37.3 us
    scatter-add x2, other arithmetic, down_step(): return acc_value.at[:, row_block, :].add(products)  20.3 us
    scatter-add x2, other arithmetic, input_step(): return acc_value.at[:, row_block, :].add(products)  20.1 us
    transpose x2, local copies, waits for them, and re-layouts, gate_up_step(): jnp.einsum('tsa,sgab->gtsb', gathered, weights[:, 0:2], preferred_element...  17.9 us
    while x3, local copies, waits for them, and re-layouts, over_blocks(): running, _ = lax.scan(advance, running, shaped)  17.3 us
    all_gather x1, waiting for transfers between devices, body(): lax.all_gather(arrived_tiles, 'dp', axis=0, tiled=True)  15.5 us
  transfers between devices with their start and end apart: 5, of which 3 were waited for; matrix products, arithmetic and copies ran while one was open for 18% of the time, Pallas kernels for 0%

commit v1 on v0

--- a/solution.py
+++ b/solution.py
@@ -4,6 +4,18 @@
 from jax.sharding import PartitionSpec as P
 
 FF = 26624
+
+
+def sent_to_each(shard, axis, split, join):
+    ways, here = (lax.axis_size(axis), lax.axis_index(axis))
+    width = shard.shape[split] // ways
+    turned = jnp.roll(shard, -here * width, axis=split)
+    got = [lax.slice_in_dim(turned, 0, width, axis=split)]
+    for far in range(1, ways):
+        sent = lax.slice_in_dim(turned, far * width, (far + 1) * width, axis=split)
+        got.append(lax.ppermute(sent, axis, [(d, (d + far) % ways) for d in range(ways)]))
+    line = jnp.concatenate(got[::-1], axis=join)
+    return jnp.roll(line, (here + 1) * got[0].shape[join], axis=join)
 
 
 def block_length(extent):
@@ -34,7 +46,7 @@
     owners = lax.axis_size("tensor")
     col_count = FF // (tile_side * owners)
     arrived_tiles, arrived_places, arrived_counts = (
-        lax.all_to_all(weight_tiles, "tensor", split_axis=0, concat_axis=0, tiled=True),
+        sent_to_each(weight_tiles, "tensor", 0, 0),
         lax.all_to_all(tile_places, "tensor", split_axis=0, concat_axis=0, tiled=True),
         lax.all_to_all(live_counts, "tensor", split_axis=0, concat_axis=0, tiled=True),
     )

time: 407 us -> 405 us (level)
  blocking collectives: 60.1 us -> 15.8 us
  waiting for transfers between devices: 70.5 us -> 102 us
  starting transfers between devices: 8.66 us -> 18 us
    all_to_all x1 -> x0, blocking collectives: 44.3 us -> none  [body(): lax.all_to_all(weight_tiles, 'tensor', split_axis=0, concat_axis=0, tiled...]
    ppermute x0 -> x7, waiting for transfers between devices: none -> 31.5 us  [sent_to_each(): lax.ppermute(sent, axis, [(d, (d + far) % ways) for d in range(ways)])]
    ppermute x0 -> x7, starting transfers between devices: none -> 7.8 us  [sent_to_each(): lax.ppermute(sent, axis, [(d, (d + far) % ways) for d in range(ways)])]
    unnamed x13 -> x20, local copies, waits for them, and re-layouts: 13.9 us -> 14.2 us
  transfers between devices with their start and end apart: 5 -> 12, of which waited for: 3 -> 7; matrix products, arithmetic and copies ran while one was open for 18% -> 19% of each run, Pallas kernels for 0% -> 0%
where the time goes in v1:
time: 405 us; the launch traced here: 403 us
  other arithmetic  115 us (28%)
  local copies, waits for them, and re-layouts  107 us (26%)
  waiting for transfers between devices  102 us (25%)
  matrix products  29.7 us (7%)
  starting transfers between devices  18 us (4%)
  blocking collectives  15.8 us (4%)
  between operations  14.7 us (4%)
    reduce_scatter x1, waiting for transfers between devices, body(): lax.psum_scatter(out_part.astype(jnp.bfloat16), 'tensor', scatter_dimensi...  51 us
    scatter-add x2, other arithmetic, gate_up_step(): return acc_value.at[:, :, col_block, :].add(products)  37.3 us
    ppermute x7, waiting for transfers between devices, sent_to_each(): lax.ppermute(sent, axis, [(d, (d + far) % ways) for d in range(ways)])  31.5 us
    scatter-add x2, other arithmetic, down_step(): return acc_value.at[:, row_block, :].add(products)  20.3 us
    scatter-add x2, other arithmetic, input_step(): return acc_value.at[:, row_block, :].add(products)  20.1 us
    transpose x2, local copies, waits for them, and re-layouts, gate_up_step(): jnp.einsum('tsa,sgab->gtsb', gathered, weights[:, 0:2], preferred_element...  18 us
    while x3, local copies, waits for them, and re-layouts, over_blocks(): running, _ = lax.scan(advance, running, shaped)  17.3 us
    all_gather x1, waiting for transfers between devices, body(): lax.all_gather(arrived_tiles, 'dp', axis=0, tiled=True)  16 us
  transfers between devices with their start and end apart: 12, of which 7 were waited for; matrix products, arithmetic and copies ran while one was open for 19% of the time, Pallas kernels for 0%

profile of v1, /device:TPU:0, one launch (start us, length us, event | category | flops | bytes accessed | tf_op | source)
XLA Modules:
  0.0 403.3 jit_solution(4191350464366508292)
XLA Ops:
  28.7 20.9 %collective-permute-done.3 = bf16[1,2,3,128,128]{4,3,2,1,0:T(8,128)(2,1)S(1)} collective-permute-done((bf16[1,2,3,128,128]{4,3,2,1,0:T(8,128)(2,1)S(1)}, bf16[1,2,3,128,128]{4,3,2,1,0:T(8,128)(2,1)S(1)}, u32[]{:S(2)}, u32[]{:S(2)}) %collective-permute-start.3) | collective-permute-done | bytes 196640 | tf_op jit(solution)/shard_map/ppermute | solution.py:16
  57.7 6.6 %copy.85 = bf16[256,8192]{0,1:T(8,128)(2,1)} copy(bf16[256,8192]{1,0:T(8,128)(2,1)} %param.17) | data formatting | bytes 8388608 | tf_op args[0]
  64.3 6.4 %copy.87 = bf16[256,64,128]{2,0,1:T(8,128)(2,1)} copy(bf16[256,64,128]{0,2,1:T(8,128)(2,1)} %bitcast.209) | data formatting | bytes 8388608 | tf_op jit(solution)/shard_map/while | solution.py:36
  70.7 6.4 %copy.90 = bf16[256,8192]{0,1:T(8,128)(2,1)} copy(bf16[256,8192]{1,0:T(8,128)(2,1)} %param.18) | data formatting | bytes 8388608 | tf_op args[1]
  77.1 6.4 %copy.92 = bf16[256,64,128]{2,0,1:T(8,128)(2,1)} copy(bf16[256,64,128]{0,2,1:T(8,128)(2,1)} %bitcast.210) | data formatting | bytes 8388608 | tf_op jit(solution)/shard_map/while | solution.py:36
  90.6 7.5 %all-reduce = s32[32]{0:T(128)S(1)} all-reduce(s32[32]{0:T(128)S(1)} %dynamic-update-slice), channel_id=3, replica_groups=mesh['dp'=4,'tensor'=8] {'dp'}, use_global_device_ids=true, to_apply=%add | all-reduce | flops 32 | bytes 256
  98.4 8.3 %all-gather = s32[32,1,2]{2,1,0:T(1,128)S(1)} all-gather(s32[8,1,2]{2,1,0:T(1,128)S(1)} %all-to-all-done), channel_id=2, replica_groups=mesh['dp'=4,'tensor'=8] {'dp'}, dimensions={0}, use_global_device_ids=true | all-gather | bytes 320 | tf_op jit(solution)/shard_map/all_gather | solution.py:55
  107.2 16.0 %all-gather.4.cloned.1.call-done = bf16[32,2,3,128,128]{4,3,2,1,0:T(8,128)(2,1)} async-done(((bf16[8,2,3,128,128]{4,3,2,1,0:T(8,128)(2,1)}), bf16[32,2,3,128,128]{4,3,2,1,0:T(8,128)(2,1)}) %all-gather.4.cloned.1.call-update) | async-done | bytes 6291472 | tf_op jit(solution)/shard_map/all_gather | solution.py:54
  134.6 74.1 %while.40 = (s32[]{:T(128)}, f32[2,256,26,128]{3,1,2,0:T(8,128)}, s32[2,32]{1,0:T(2,128)S(1)}, bf16[2,32,3,128,128]{4,3,2,1,0:T(8,128)(2,1)}, s32[2,32]{1,0:T(2,...) while((s32[]{:T(128)}, f32[2,256,26,128]{3,1,2,0:T(8,128)}, s32[2,32]{1,0:T(2,128)S(1)}, ...), condition=%wide.region_2.5_spmd, body=%wide.region_0.4_spmd.sunk | while | flops 540017984 | bytes 59774484 | solution.py:36
  144.0 9.0 %copy.102 = f32[32,2,256,128]{3,2,1,0:T(8,128)} copy(f32[32,2,256,128]{2,3,1,0:T(8,128)} %convolution_bitcast_fusion.2) | data formatting | bytes 16777216 | tf_op jit(solution)/shard_map/while/body/eval_jaxpr/tsa,sgab->gtsb/transpose | solution.py:72
  153.0 18.7 %scatter_fusion = f32[2,256,26,128]{3,1,2,0:T(8,128)} fusion(f32[2,256,26,128]{3,1,2,0:T(8,128)} %get-tuple-element.484, s32[32]{0:T(128)S(1)} %fusion.71, f32[32,2,256,128]{3,2,1,0:T(8,128)} %copy.102), kind=kCustom, calls=%fused_computation.4.clone.1 | custom fusion | flops 2097152 | bytes 25165952 | tf_op jit(solution)/shard_map/while/body/eval_jaxpr/scatter-add | solution.py:75
  174.9 6.2 %convolution_bitcast_fusion.2 = f32[32,2,256,128]{2,3,1,0:T(8,128)} fusion(bf16[2,32,3,128,128]{4,3,2,1,0:T(8,128)(2,1)} %get-tuple-element.493, s32[]{:T(128)} %get-tuple-element.483, bf16[32,256,128]{2,1,0:T(8,128)(2,1)S(1)} %gather_fusion, pred[32]{0:T(512)(128)(4,1)S(1)} %get-tuple-element.451), kind=kOutput, calls=%fused_computation.45.clone.1 | convolution fusion | flops 537919488 | bytes 13632032 | tf_op jit(solution)/shard_map/while/body/eval_jaxpr/tsa,sgab->gtsb/dot_general | solution.py:72
  181.1 9.0 %copy.102 = f32[32,2,256,128]{3,2,1,0:T(8,128)} copy(f32[32,2,256,128]{2,3,1,0:T(8,128)} %convolution_bitcast_fusion.2) | data formatting | bytes 16777216 | tf_op jit(solution)/shard_map/while/body/eval_jaxpr/tsa,sgab->gtsb/transpose | solution.py:72
  190.1 18.6 %scatter_fusion = f32[2,256,26,128]{3,1,2,0:T(8,128)} fusion(f32[2,256,26,128]{3,1,2,0:T(8,128)} %get-tuple-element.484, s32[32]{0:T(128)S(1)} %fusion.71, f32[32,2,256,128]{3,2,1,0:T(8,128)} %copy.102), kind=kCustom, calls=%fused_computation.4.clone.1 | custom fusion | flops 2097152 | bytes 25165952 | tf_op jit(solution)/shard_map/while/body/eval_jaxpr/scatter-add | solution.py:75
  209.0 32.3 %while.42 = (s32[]{:T(128)}, f32[256,26,128]{2,0,1:T(8,128)S(1)}, s32[2,32]{1,0:T(2,128)S(1)}, bf16[2,32,3,128,128]{4,3,1,2,0:T(8,128)(2,1)}, s32[2,32]{1,0:T(2,...) while((s32[]{:T(128)}, f32[256,26,128]{2,0,1:T(8,128)S(1)}, s32[2,32]{1,0:T(2,128)S(1)}, ...), condition=%wide.region_9.12_spmd, body=%wide.region_7.11_spmd.sunk | while | flops 270533920 | bytes 38802964 | solution.py:36
  218.7 6.5 %scatter_fusion.2 = f32[256,26,128]{2,0,1:T(8,128)S(1)} fusion(f32[256,26,128]{2,0,1:T(8,128)S(1)} %get-tuple-element.505, s32[32]{0:T(128)S(1)} %fusion.76, f32[32,256,128]{2,1,0:T(8,128)} %fusion.77), kind=kCustom, calls=%fused_computation.7.clone.1 | custom fusion | flops 1048576 | bytes 12583040 | tf_op jit(solution)/shard_map/while/body/eval_jaxpr/scatter-add | solution.py:108
  234.8 6.5 %scatter_fusion.2 = f32[256,26,128]{2,0,1:T(8,128)S(1)} fusion(f32[256,26,128]{2,0,1:T(8,128)S(1)} %get-tuple-element.505, s32[32]{0:T(128)S(1)} %fusion.76, f32[32,256,128]{2,1,0:T(8,128)} %fusion.77), kind=kCustom, calls=%fused_computation.7.clone.1 | custom fusion | flops 1048576 | bytes 12583040 | tf_op jit(solution)/shard_map/while/body/eval_jaxpr/scatter-add | solution.py:108
  250.8 39.0 %while.43 = (s32[]{:T(128)}, f32[256,64,128]{2,0,1:T(8,128)}, s32[2,32]{1,0:T(2,128)S(1)}, bf16[2,32,3,128,128]{4,3,2,1,0:T(8,128)(2,1)}, s32[2,32]{1,0:T(2,128)...) while((s32[]{:T(128)}, f32[256,64,128]{2,0,1:T(8,128)}, s32[2,32]{1,0:T(2,128)S(1)}, ...), condition=%wide.region_12.15_spmd, body=%wide.region_10.14_spmd.sunk | while | flops 540018048 | bytes 54531732 | solution.py:36
  260.3 10.1 %scatter_fusion.3 = f32[256,64,128]{2,0,1:T(8,128)} fusion(f32[256,64,128]{2,0,1:T(8,128)} %get-tuple-element.547, s32[32]{0:T(128)S(1)} %get-tuple-element.474, f32[32,256,128]{2,1,0:T(8,128)} %fusion.81), kind=kCustom, calls=%fused_computation.6.clone.1 | custom fusion | flops 1048576 | bytes 12583040 | tf_op jit(solution)/shard_map/while/body/eval_jaxpr/scatter-add | solution.py:125
  279.8 10.0 %scatter_fusion.3 = f32[256,64,128]{2,0,1:T(8,128)} fusion(f32[256,64,128]{2,0,1:T(8,128)} %get-tuple-element.547, s32[32]{0:T(128)S(1)} %get-tuple-element.474, f32[32,256,128]{2,1,0:T(8,128)} %fusion.81), kind=kCustom, calls=%fused_computation.6.clone.1 | custom fusion | flops 1048576 | bytes 12583040 | tf_op jit(solution)/shard_map/while/body/eval_jaxpr/scatter-add | solution.py:125
  300.4 35.5 %while.41 = (s32[]{:T(128)}, f32[256,64,128]{2,0,1:T(8,128)}, s32[2,32]{1,0:T(2,128)S(1)}, bf16[2,32,3,128,128]{4,3,1,2,0:T(8,128)(2,1)}, s32[2,32]{1,0:T(2,128)S(1)}, /*index=5*/bf16[256,26,128]{2,0,1:T(8,128)(2,1)}, s32[]{:T(128)}) while((s32[]{:T(128)}, f32[256,64,128]{2,0,1:T(8,128)}, s32[2,32]{1,0:T(2,128)S(1)}, ...), condition=%wide.region_5.8_spmd, body=%wide.region_3.7_spmd.sunk | while | flops 270534016 | bytes 30414456 | solution.py:36
  308.1 10.2 %scatter_fusion.1 = f32[256,64,128]{2,0,1:T(8,128)} fusion(f32[256,64,128]{2,0,1:T(8,128)} %get-tuple-element.526, s32[32]{0:T(128)S(1)} %get-tuple-element.458, f32[32,256,128]{2,1,0:T(8,128)} %fusion.74), kind=kCustom, calls=%fused_computation.5.clone.1 | custom fusion | flops 1048576 | bytes 12583040 | tf_op jit(solution)/shard_map/while/body/eval_jaxpr/scatter-add | solution.py:92
  325.8 10.1 %scatter_fusion.1 = f32[256,64,128]{2,0,1:T(8,128)} fusion(f32[256,64,128]{2,0,1:T(8,128)} %get-tuple-element.526, s32[32]{0:T(128)S(1)} %get-tuple-element.458, f32[32,256,128]{2,1,0:T(8,128)} %fusion.74), kind=kCustom, calls=%fused_computation.5.clone.1 | custom fusion | flops 1048576 | bytes 12583040 | tf_op jit(solution)/shard_map/while/body/eval_jaxpr/scatter-add | solution.py:92
  345.7 51.0 %reduce-scatter.3.cloned.1.call-done = bf16[256,1024]{1,0:T(8,128)(2,1)} async-done(((bf16[256,8192]{1,0:T(8,128)(2,1)}), bf16[256,1024]{1,0:T(8,128)(2,1)}) %reduce-scatter.3.cloned.1.call-update) | async-done | bytes 524304 | tf_op jit(solution)/shard_map/reduce_scatter | solution.py:97
  (124 shorter events, 143.8 us)
Async XLA Ops:
  7.2 116.0 %all-gather.4.cloned.1.call-start = ((), (), s32[]{:S(2)}) async-start(), calls=%async_computation.4 | async-start | bytes 7864320 | tf_op jit(solution)/shard_map/all_gather | solution.py:54
  10.1 10.1 %collective-permute-start = (bf16[1,2,3,128,128]{4,3,2,1,0:T(8,128)(2,1)}, bf16[1,2,3,128,128]{4,3,2,1,0:T(8,128)(2,1)S(1)}, u32[]{:S(2)}, u32[]{:S(2)}) collective-permute-start(bf16[1,2,3,128,128]{4,3,2,1,0:T(8,128)(2,1)} %get-tuple-element.309), channel_id=1, source_target_pairs={{0,7},{1,0},{2,1},{3,2},{4,3},{5,4},{6,5},{7,6},{8,15},{9,8},{10,9... | collective-permute-start | bytes 589832 | tf_op jit(solution)/shard_map/ppermute | solution.py:16
  14.6 9.9 %collective-permute-start.1 = (bf16[1,2,3,128,128]{4,3,2,1,0:T(8,128)(2,1)}, bf16[1,2,3,128,128]{4,3,2,1,0:T(8,128)(2,1)S(1)}, u32[]{:S(2)}, u32[]{:S(2)}) collective-permute-start(bf16[1,2,3,128,128]{4,3,2,1,0:T(8,128)(2,1)} %get-tuple-element.308), channel_id=1, source_target_pairs={{0,6},{1,7},{2,0},{3,1},{4,2},{5,3},{6,4},{7,5},{8,14},{9,15},{10,... | collective-permute-start | bytes 589832 | tf_op jit(solution)/shard_map/ppermute | solution.py:16
  15.1 13.5 %collective-permute-start.2 = (bf16[1,2,3,128,128]{4,3,2,1,0:T(8,128)(2,1)S(1)}, bf16[1,2,3,128,128]{4,3,2,1,0:T(8,128)(2,1)S(1)}, u32[]{:S(2)}, u32[]{:S(2)}) collective-permute-start(bf16[1,2,3,128,128]{4,3,2,1,0:T(8,128)(2,1)S(1)} %get-tuple-element.307), channel_id=1, source_target_pairs={{0,5},{1,6},{2,7},{3,0},{4,1},{5,2},{6,3},{7,4},{8,13},{9,14},{10,... | collective-permute-start | bytes 589832 | tf_op jit(solution)/shard_map/ppermute | solution.py:16
  15.1 34.4 %collective-permute-start.3 = (bf16[1,2,3,128,128]{4,3,2,1,0:T(8,128)(2,1)S(1)}, bf16[1,2,3,128,128]{4,3,2,1,0:T(8,128)(2,1)S(1)}, u32[]{:S(2)}, u32[]{:S(2)}) collective-permute-start(bf16[1,2,3,128,128]{4,3,2,1,0:T(8,128)(2,1)S(1)} %get-tuple-element.306), channel_id=1, source_target_pairs={{0,4},{1,5},{2,6},{3,7},{4,0},{5,1},{6,2},{7,3},{8,12},{9,13},{10,... | collective-permute-start | bytes 589832 | tf_op jit(solution)/shard_map/ppermute | solution.py:16
  17.9 31.7 %collective-permute-start.4 = (bf16[1,2,3,128,128]{4,3,2,1,0:T(8,128)(2,1)S(1)}, bf16[1,2,3,128,128]{4,3,2,1,0:T(8,128)(2,1)S(1)}, u32[]{:S(2)}, u32[]{:S(2)}) collective-permute-start(bf16[1,2,3,128,128]{4,3,2,1,0:T(8,128)(2,1)S(1)} %get-tuple-element.305), channel_id=1, source_target_pairs={{0,3},{1,4},{2,5},{3,6},{4,7},{5,0},{6,1},{7,2},{8,11},{9,12},{10,... | collective-permute-start | bytes 589832 | tf_op jit(solution)/shard_map/ppermute | solution.py:16
  20.2 29.4 %collective-permute-start.5 = (bf16[1,2,3,128,128]{4,3,2,1,0:T(8,128)(2,1)S(1)}, bf16[1,2,3,128,128]{4,3,2,1,0:T(8,128)(2,1)S(1)}, u32[]{:S(2)}, u32[]{:S(2)}) collective-permute-start(bf16[1,2,3,128,128]{4,3,2,1,0:T(8,128)(2,1)S(1)} %get-tuple-element.304), channel_id=1, source_target_pairs={{0,2},{1,3},{2,4},{3,5},{4,6},{5,7},{6,0},{7,1},{8,10},{9,11},{10,... | collective-permute-start | bytes 589832 | tf_op jit(solution)/shard_map/ppermute | solution.py:16
  24.5 25.2 %collective-permute-start.6 = (bf16[1,2,3,128,128]{4,3,2,1,0:T(8,128)(2,1)S(1)}, bf16[1,2,3,128,128]{4,3,2,1,0:T(8,128)(2,1)S(1)}, u32[]{:S(2)}, u32[]{:S(2)}) collective-permute-start(bf16[1,2,3,128,128]{4,3,2,1,0:T(8,128)(2,1)S(1)} %get-tuple-element.303), channel_id=1, source_target_pairs={{0,1},{1,2},{2,3},{3,4},{4,5},{5,6},{6,7},{7,0},{8,9},{9,10},{10,1... | collective-permute-start | bytes 589832 | tf_op jit(solution)/shard_map/ppermute | solution.py:16
  28.6 22.9 %copy-start.4 = (s32[8]{0:T(128)S(1)}, s32[8]{0:T(128)}, u32[]{:S(2)}) copy-start(s32[8]{0:T(128)} %param.21) | copy-start | bytes 100
  28.6 28.3 %copy-start.3 = (s32[8,2]{0,1:T(2,128)S(1)}, s32[8,2]{0,1:T(2,128)}, u32[]{:S(2)}) copy-start(s32[8,2]{0,1:T(2,128)} %param.20) | copy-start | bytes 196
  52.2 32.7 %all-to-all-start.1 = ((s32[8,1,1]{2,1,0:T(1,128)}), s32[8,1,1]{2,1,0:T(1,128)S(1)}, u32[]{:S(2)}, u32[]{:S(2)}) async-start(s32[8,1,1]{2,1,0:T(1,128)} %copy.83), calls=%async_computation.1 | async-start | bytes 8192 | tf_op jit(solution)/shard_map/all_to_all | solution.py:51
  77.1 6.4 %copy-start.5 = (u32[32]{0:T(128)S(1)}, u32[32]{0:T(128)}, u32[]{:S(2)}) copy-start(u32[32]{0:T(128)} %constant.142) | copy-start | bytes 388
  84.9 13.4 %all-to-all-start = ((s32[8,1,2]{2,1,0:T(1,128)}), s32[8,1,2]{2,1,0:T(1,128)S(1)}, u32[]{:S(2)}, u32[]{:S(2)}) async-start(s32[8,1,2]{2,1,0:T(1,128)} %copy.78), calls=%async_computation | async-start | bytes 8192 | tf_op jit(solution)/shard_map/all_to_all | solution.py:50
  90.1 255.7 %reduce-scatter.5.cloned.1.call-start = ((), (), s32[]{:S(2)}) async-start(), calls=%async_computation.6 | async-start | bytes 4718592 | tf_op jit(solution)/shard_map/reduce_scatter | solution.py:130
  126.4 4.5 %copy-start = (bf16[2,32,3,128,128]{4,3,2,1,0:T(8,128)(2,1)}, bf16[2,32,3,128,128]{4,3,2,1,0:T(8,128)(2,1)S(1)}, u32[]{:S(2)}) copy-start(bf16[2,32,3,128,128]{4,3,2,1,0:T(8,128)(2,1)S(1)} %bitcast_select_fusion) | copy-start | bytes 18874372
  213.4 2.5 copy-start.1
  229.6 2.5 copy-start.1
  253.9 3.1 copy-start.2
  273.4 3.1 copy-start.2
  295.9 100.9 %reduce-scatter.3.cloned.1.call-start = ((), (), s32[]{:S(2)}) async-start(), calls=%async_computation.5 | async-start | bytes 4718592 | tf_op jit(solution)/shard_map/reduce_scatter | solution.py:97
Sparse Core Ops, SparseCore 0:
  51.6 71.4 all-gather.3
  296.0 49.6 reduce-scatter.4
  348.6 48.1 reduce-scatter.2
